TPU v7x, 32 devices: a whole 2x2x4 slice. The times are simulated.
32 devices in a mesh: req: 8 (over y, x, core), head: 4 (over z).
Axes of the slice: x: 2, y: 2, z: 4, core: 2. Of those that a mesh axis runs over, the one named last changes fastest.
Arguments:
- prefill_query: bfloat16 [4096, 2048], P('req', 'head'), may hold values from -16 to 16
- prefill_new_pairs: bfloat16 [4096, 2, 1024], P('req', None, 'head'), may hold values from -16 to 16
- prefill_cache: bfloat16 [8, 2, 2048, 1024], P('req', None, None, 'head'), may hold values from -16 to 16
- prefill_start: int32 [8], P('req'), may hold values from 0 to 2048, as said below
- decode_query: bfloat16 [24, 2048], P('req', 'head'), may hold values from -16 to 16
- decode_fresh: bfloat16 [24, 2, 1024], P('req', None, 'head'), may hold values from -16 to 16
- decode_cache: bfloat16 [24, 2, 2048, 1024], P('req', None, None, 'head'), may hold values from -16 to 16
- decode_length: int32 [24], P('req'), may hold values from 2 to 2048
- decode_slot: int32 [24], P('req'), may hold values from 0 to 23, each once
- prefill_states: bfloat16 [4096, 2048], P('req', 'head'), may hold values from -32 to 32
- decode_states: bfloat16 [24, 2048], P('req', 'head'), may hold values from -32 to 32
- output_proj: bfloat16 [2048, 2048], P('head', 'req'), may hold values from -0.125 to 0.125
- norm_gain: bfloat16 [2048], replicated, may hold values from 0.099609375 to 1.8984375
- gate_weight: bfloat16 [2048, 6144], P('req', 'head'), may hold values from -0.125 to 0.125
- up_weight: bfloat16 [2048, 6144], P('req', 'head'), may hold values from -0.125 to 0.125
- down_weight: bfloat16 [6144, 2048], P('head', 'req'), may hold values from -0.078125 to 0.078125
Outputs:
- prefill_result: bfloat16 [4096, 2048], P('req', 'head')
- decode_result: bfloat16 [24, 2048], P('req', 'head')
Inputs may be any that keep to these rules, and one draw needn't show every extreme that they name: `decode_slot`: a permutation; the cache of slot s is held by req index s // 3. `prefill_start`: a multiple of 512.
All inputs are finite; a program needn't handle non-finite values.
Results may differ from a plain program's by a relative error of at most 0.0094.
Values may be sent and summed in bfloat16 or wider, within the bound.
A program may use at most 128 MiB of HBM per device.

v0:
```python
import math

import jax
import jax.numpy as jnp
from jax import lax
from jax.sharding import PartitionSpec as P

HEAD_SIZE = 128
REQUEST_TOKENS = 512


rope_base = 1000000.0
norm_eps = 1e-06


def rope_tables(positions, head_size):
    half_size = head_size // 2
    lane_index = jnp.arange(half_size, dtype=jnp.float32)
    inverse = jnp.power(jnp.float32(rope_base), -2.0 * lane_index / head_size)
    angles = positions.astype(jnp.float32)[:, None] * inverse[None, :]
    cosine = jnp.concatenate([jnp.cos(angles), jnp.cos(angles)], axis=1)
    sine_table = jnp.concatenate([jnp.sin(angles), jnp.sin(angles)], axis=1)
    return (cosine, sine_table)


def rotate(vectors, cosine, sine_table):
    half_size = vectors.shape[-1] // 2
    front_half = vectors[..., :half_size]
    back_half = vectors[..., half_size:]
    turned = jnp.concatenate([-back_half, front_half], axis=-1)
    return vectors * cosine[:, None, :] + turned * sine_table[:, None, :]


def attend(query_rows, key_rows, value_rows, visible):
    row_count, head_count, head_size = query_rows.shape
    groups = key_rows.shape[1]
    grouped = query_rows.reshape(row_count, groups, head_count // groups, head_size)
    scores = jnp.einsum("qhgd,khd->hgqk", grouped, key_rows, preferred_element_type=jnp.float32) * (
        1.0 / math.sqrt(head_size)
    )
    scores = jnp.where(visible[None, None], scores, -jnp.inf)
    highest = jnp.max(scores, axis=-1, keepdims=True)
    unnormed = jnp.exp(scores - highest)
    totals = jnp.sum(unnormed, axis=-1, keepdims=True)
    rounded = unnormed.astype(jnp.bfloat16)
    blended = jnp.einsum("hgqk,khd->qhgd", rounded, value_rows, preferred_element_type=jnp.float32)
    blended = blended / jnp.transpose(totals, (2, 0, 1, 3))
    return blended.reshape(row_count, head_count * head_size).astype(jnp.bfloat16)


def prefill_task(query_rows, fresh_rows, cache_rows, offset_value, head_size):
    span_len = query_rows.shape[0]
    positions = offset_value + jnp.arange(span_len, dtype=jnp.int32)
    cosine, sine_table = rope_tables(positions, head_size)
    head_count = query_rows.shape[1] // head_size
    groups = fresh_rows.shape[2] // head_size
    rot_query = rotate(
        query_rows.astype(jnp.float32).reshape(span_len, head_count, head_size), cosine, sine_table
    ).astype(jnp.bfloat16)
    rot_key = rotate(
        fresh_rows[:, 0].astype(jnp.float32).reshape(span_len, groups, head_size),
        cosine,
        sine_table,
    ).astype(jnp.bfloat16)
    cache_len = cache_rows.shape[1]
    key_rows = jnp.concatenate(
        [cache_rows[0].reshape(cache_len, groups, head_size), rot_key], axis=0
    )
    value_rows = jnp.concatenate(
        [
            cache_rows[1].reshape(cache_len, groups, head_size),
            fresh_rows[:, 1].reshape(span_len, groups, head_size),
        ],
        axis=0,
    )
    cache_seen = jnp.broadcast_to(
        jnp.arange(cache_len, dtype=jnp.int32)[None, :] < offset_value, (span_len, cache_len)
    )
    own_seen = (
        jnp.arange(span_len, dtype=jnp.int32)[None, :]
        <= jnp.arange(span_len, dtype=jnp.int32)[:, None]
    )
    visible = jnp.concatenate([cache_seen, own_seen], axis=1)
    return attend(rot_query, key_rows, value_rows, visible)


def decode_task(query_rows, fresh_rows, cache_rows, length, head_size):
    positions = jnp.reshape(length, (1,))
    cosine, sine_table = rope_tables(positions, head_size)
    head_count = query_rows.shape[0] // head_size
    groups = fresh_rows.shape[1] // head_size
    rot_query = rotate(
        query_rows.astype(jnp.float32).reshape(1, head_count, head_size), cosine, sine_table
    ).astype(jnp.bfloat16)
    rot_key = rotate(
        fresh_rows[0].astype(jnp.float32).reshape(1, groups, head_size), cosine, sine_table
    ).astype(jnp.bfloat16)
    cache_len = cache_rows.shape[1]
    key_rows = jnp.concatenate(
        [cache_rows[0].reshape(cache_len, groups, head_size), rot_key], axis=0
    )
    value_rows = jnp.concatenate(
        [
            cache_rows[1].reshape(cache_len, groups, head_size),
            fresh_rows[1].reshape(1, groups, head_size),
        ],
        axis=0,
    )
    visible = jnp.concatenate(
        [jnp.arange(cache_len, dtype=jnp.int32)[None, :] < length, jnp.ones((1, 1), jnp.bool_)],
        axis=1,
    )
    return attend(rot_query, key_rows, value_rows, visible)[0]


def decode_attend(own_query, own_fresh, decode_cache, decode_length):

    def one_slot(query_rows, fresh_rows, cache_rows, length):
        return decode_task(query_rows, fresh_rows, cache_rows, length, HEAD_SIZE)

    return jax.vmap(one_slot)(own_query, own_fresh, decode_cache, decode_length)


def body(
    prefill_query,
    prefill_new_pairs,
    prefill_cache,
    prefill_start,
    decode_query,
    decode_fresh,
    decode_cache,
    decode_length,
    decode_slot,
    prefill_states,
    decode_states,
    output_proj,
    norm_gain,
    gate_weight,
    up_weight,
    down_weight,
):
    local_prefills = prefill_query.shape[0] // REQUEST_TOKENS
    query_blocks = prefill_query.reshape(local_prefills, REQUEST_TOKENS, prefill_query.shape[1])
    newest_blocks = prefill_new_pairs.reshape(
        local_prefills, REQUEST_TOKENS, 2, prefill_new_pairs.shape[2]
    )
    prefill_att = lax.map(
        lambda operands: prefill_task(
            operands[0], operands[1], operands[2], operands[3], HEAD_SIZE
        ),
        (query_blocks, newest_blocks, prefill_cache, prefill_start),
    )
    prefill_att = prefill_att.reshape(local_prefills * REQUEST_TOKENS, prefill_query.shape[1])
    local_decodes = decode_query.shape[0]
    fresh_width = decode_fresh.shape[2]
    fresh_flat = decode_fresh.reshape(local_decodes, 2 * fresh_width)
    slot_marks = decode_slot.astype(jnp.bfloat16)
    every_query, every_fresh, every_slot = (
        lax.all_gather(decode_query, "req", axis=0, tiled=True),
        lax.all_gather(fresh_flat, "req", axis=0, tiled=True),
        lax.all_gather(slot_marks, "req", axis=0, tiled=True),
    )
    owned = lax.axis_index("req") * local_decodes + jnp.arange(local_decodes, dtype=jnp.int32)
    picker = (every_slot.astype(jnp.int32)[None, :] == owned[:, None]).astype(jnp.bfloat16)
    own_query = jnp.dot(picker, every_query, preferred_element_type=jnp.float32).astype(
        jnp.bfloat16
    )
    own_fresh = jnp.dot(picker, every_fresh, preferred_element_type=jnp.float32).astype(
        jnp.bfloat16
    )
    own_att = decode_attend(
        own_query, own_fresh.reshape(local_decodes, 2, fresh_width), decode_cache, decode_length
    )
    every_att = lax.all_gather(own_att, "req", axis=0, tiled=True)
    total_slots = every_att.shape[0]
    chooser = (decode_slot[:, None] == jnp.arange(total_slots, dtype=jnp.int32)[None, :]).astype(
        jnp.bfloat16
    )
    decode_att = jnp.dot(chooser, every_att, preferred_element_type=jnp.float32).astype(
        jnp.bfloat16
    )
    attended = jnp.concatenate([prefill_att, decode_att], axis=0)
    states = jnp.concatenate([prefill_states, decode_states], axis=0)
    partial_value = jnp.dot(
        attended,
        lax.all_gather(output_proj, "req", axis=1, tiled=True),
        preferred_element_type=jnp.float32,
    )
    model_width = partial_value.shape[1]
    share_cols = model_width // lax.axis_size("head")
    share_start = lax.axis_index("head") * share_cols
    summed = lax.psum_scatter(
        partial_value, "head", scatter_dimension=1, tiled=True
    ) + states.astype(jnp.float32)
    squares = lax.psum(jnp.sum(summed * summed, axis=1), "head")
    gain_share = lax.dynamic_slice_in_dim(norm_gain, share_start, share_cols, 0).astype(jnp.float32)
    normed_share = (
        summed * lax.rsqrt(squares[:, None] / model_width + norm_eps) * gain_share
    ).astype(jnp.bfloat16)
    normed = lax.all_gather(normed_share, "head", axis=1, tiled=True)

    def add_rows(weight_piece):
        return jnp.dot(normed, weight_piece, preferred_element_type=jnp.float32)

    gate_sum = add_rows(lax.all_gather(gate_weight, "req", axis=0, tiled=True))
    upper = add_rows(lax.all_gather(up_weight, "req", axis=0, tiled=True))
    hidden = (jax.nn.silu(gate_sum) * upper).astype(jnp.bfloat16)
    down_terms = jnp.dot(
        hidden,
        lax.all_gather(down_weight, "req", axis=1, tiled=True),
        preferred_element_type=jnp.float32,
    )
    result = (
        summed + lax.psum_scatter(down_terms, "head", scatter_dimension=1, tiled=True)
    ).astype(jnp.bfloat16)
    prefill_rows = prefill_att.shape[0]
    return (result[:prefill_rows], result[prefill_rows:])


def solution(mesh):
    in_specs = (
        P("req", "head"),
        P("req", None, "head"),
        P("req", None, None, "head"),
        P("req"),
        P("req", "head"),
        P("req", None, "head"),
        P("req", None, None, "head"),
        P("req"),
        P("req"),
        P("req", "head"),
        P("req", "head"),
        P("head", "req"),
        P(),
        P("req", "head"),
        P("req", "head"),
        P("head", "req"),
    )
    out_specs = (P("req", "head"), P("req", "head"))
    return jax.shard_map(body, mesh=mesh, in_specs=in_specs, out_specs=out_specs, check_vma=False)
```

profile of v0, /device:TPU:0, one launch (start us, length us, event | category | flops | bytes accessed | tf_op | source)
XLA Modules:
  0.0 508.4 jit_solution(15128024461800566149)
XLA Ops:
  7.2 0.7 all-gather.9.cloned.1.call-update
  8.0 0.8 iota_compare_fusion
  8.8 1.3 copy.66
  10.0 0.7 convert_element_type.153
  10.7 1.2 dynamic-slice.2
  12.6 0.2 dynamic-update-slice
  12.8 2.6 reshape.328
  15.5 15.3 %all-reduce.1 = bf16[24]{0:T(256)(128)(2,1)S(1)} all-reduce(bf16[24]{0:T(256)(128)(2,1)S(1)} %dynamic-update-slice), channel_id=1, replica_groups=mesh['req'=8,'head'=4] {'req'}, use_global_device_ids=true, to_apply=%add.1 | all-reduce | flops 24 | bytes 96
  30.8 8.0 %all-gather.1 = bf16[8,3,512]{2,1,0:T(4,128)(2,1)S(1)} all-gather(bf16[1,3,512]{2,1,0:T(4,128)(2,1)S(1)} %bitcast.120), channel_id=1, replica_groups=mesh['req'=8,'head'=4] {'req'}, dimensions={0}, use_global_device_ids=true | all-gather | bytes 27648 | tf_op jit(solution)/shard_map/all_gather | solution.py:159
  38.8 0.2 fusion.31
  39.8 1.5 fusion.88
  41.3 0.7 copy.79
  42.0 0.1 copy.61
  42.2 1.1 slice_negate_fusion.1
  43.3 1.0 copy-done.10
  44.3 1.5 fusion.87
  45.8 1.5 copy.78
  47.3 1.3 copy.64
  48.6 0.1 slice_negate_fusion
  48.8 1.4 copy.67
  50.2 1.4 copy.68
  51.6 1.4 copy.57
  53.0 1.3 copy.58
  54.4 9.3 %all-gather = bf16[8,3,512]{2,1,0:T(4,128)(2,1)S(1)} all-gather(bf16[1,3,512]{2,1,0:T(4,128)(2,1)S(1)} %reshape.334), channel_id=1, replica_groups=mesh['req'=8,'head'=4] {'req'}, dimensions={0}, use_global_device_ids=true | all-gather | bytes 27648 | tf_op jit(solution)/shard_map/all_gather | solution.py:160
  63.7 0.2 convolution_convert_fusion.2
  64.0 1.7 multiply_cosine_fusion
  65.7 0.1 multiply_cosine_fusion.1
  65.9 5.8 %fusion.86 = (bf16[3,1,2048,256]{3,2,1,0:T(8,128)(2,1)}, bf16[3,1,2048,256]{3,2,1,0:T(8,128)(2,1)}) fusion(bf16[3,2,2048,256]{3,2,1,0:T(8,128)(2,1)} %param.22), kind=kLoop, calls=%fused_computation.112 | loop fusion | bytes 12582912 | tf_op jit(solution)/shard_map/vmap()/slice | solution.py:100
  71.7 3.2 copy.81
  74.9 2.8 copy.73
  77.8 3.2 copy.80
  81.0 2.8 copy.71
  84.0 3.1 fusion.89
  87.1 0.2 fusion.56
  87.3 0.6 fusion.41
  88.0 8.3 %all-gather.2 = bf16[8,3,512]{2,1,0:T(4,128)(2,1)S(1)} all-gather(bf16[1,3,512]{2,1,0:T(4,128)(2,1)S(1)} %reshape.338), channel_id=1, replica_groups=mesh['req'=8,'head'=4] {'req'}, dimensions={0}, use_global_device_ids=true | all-gather | bytes 27648 | tf_op jit(solution)/shard_map/all_gather | solution.py:174
  96.3 0.2 convolution_convert_fusion
  96.5 0.2 copy.74
  96.7 1.4 pad_maximum_fusion
  98.1 1.9 pad_add_fusion
  99.9 1.3 fusion.53
  101.3 10.0 %fusion.2 = (f32[2,2,512]{2,1,0:T(2,128)S(1)}, f32[2,2560,512,2]{2,1,3,0:T(8,128)}) fusion(pred[512,2560]{0,1:T(8,128)(4,1)S(1)} %pad_add_fusion, f32[512,2,2,64]{3,0,2,1:T(8,128)S(1)} %copy-done.7, f32[512,2,2,64]{3,0,2,1:T(8,128)S(1)} %copy-done.6, f32[512,2,2,128]{3,2,1,0:T(2,128)S(1)} %copy-done.4, f32[512,128]{1,0:T(8,128)S(1)} %get-tuple-element.47, ...), kind=kOutput, calls=%fused_computation.4 | convolution fusion | flops 1361836032 | bytes 26222592 | tf_op jit(solution)/shard_map/while/body/eval_jaxpr/qhgd,khd->hgqk/dot_general | solution.py:38
  111.3 9.6 %fusion = f32[2,2,512]{2,1,0:T(2,128)S(1)} fusion(f32[2,2560,512,2]{2,1,3,0:T(8,128)} %get-tuple-element.43, f32[2,2,512]{2,1,0:T(2,128)S(1)} %get-tuple-element.42, pred[512,2560]{0,1:T(8,128)(4,1)S(1)} %pad_add_fusion), kind=kLoop, calls=%fused_computation.2 | loop fusion | flops 20969472 | bytes 22298624 | tf_op jit(solution)/shard_map/while/body/eval_jaxpr/reduce_sum | solution.py:44
  120.9 10.4 %fusion.28 = bf16[512,2,2,128]{0,3,2,1:T(8,128)(2,1)S(1)} fusion(f32[2,2560,512,2]{2,1,3,0:T(8,128)} %get-tuple-element.43, f32[2,2,512]{2,1,0:T(2,128)S(1)} %get-tuple-element.42, pred[512,2560]{0,1:T(8,128)(4,1)S(1)} %pad_add_fusion, bf16[512,2,128]{0,2,1:T(8,128)(2,1)S(1)} %bitcast.116, bf16[2048,2,128]{0,2,1:T(8,128)(2,1)S(1)} %bitcast.114, ...), kind=kOutput, calls=%fused_computation.30 | convolution fusion | flops 1366294528 | bytes 24133632 | tf_op jit(solution)/shard_map/while/body/eval_jaxpr/hgqk,khd->qhgd/dot_general | solution.py:46
  131.3 5.0 fusion.47
  136.4 0.7 all-gather.13.cloned.1.call-update
  137.1 0.8 dynamic-slice_convert_fusion
  137.9 76.8 %reduce-scatter.3.cloned.1.call-done = f32[515,512]{1,0:T(8,128)} async-done(((f32[515,2048]{1,0:T(8,128)}), f32[515,512]{1,0:T(8,128)}) %reduce-scatter.3.cloned.1.call-update) | async-done | bytes 1054736 | tf_op jit(solution)/shard_map/reduce_scatter | solution.py:192
  214.7 1.5 multiply_reduce_fusion
  216.2 10.9 %psum.7 = f32[515]{0:T(1024)S(1)} all-reduce(f32[515]{0:T(1024)S(1)} %multiply_reduce_fusion), channel_id=1, replica_groups=mesh['req'=8,'head'=4] {'head'}, use_global_device_ids=true, to_apply=%region_6.7 | all-reduce | flops 515 | bytes 4120 | tf_op jit(solution)/shard_map/psum | solution.py:195
  227.1 2.2 multiply_convert_fusion
  229.4 0.5 all-gather.15.cloned.1.call-update
  230.0 0.5 all-gather.17.cloned.1.call-update
  230.5 0.3 reduce-scatter.5.cloned.1.call-start
  230.8 32.0 %all-gather.13.cloned.1.call-done = bf16[2048,1536]{1,0:T(8,128)(2,1)} async-done(((bf16[256,1536]{1,0:T(8,128)(2,1)}), bf16[2048,1536]{1,0:T(8,128)(2,1)}) %all-gather.13.cloned.1.call-update) | async-done | bytes 6291472 | tf_op jit(solution)/shard_map/all_gather | solution.py:205
  262.8 48.1 %all-gather.11.cloned.1.call-done = bf16[515,2048]{1,0:T(8,128)(2,1)} async-done(((bf16[515,512]{1,0:T(8,128)(2,1)}), bf16[515,2048]{1,0:T(8,128)(2,1)}) %all-gather.11.cloned.1.call-update) | async-done | bytes 2109456 | tf_op jit(solution)/shard_map/all_gather | solution.py:200
  311.0 8.6 %fusion.90 = f32[515,1536]{1,0:T(8,128)} fusion(bf16[515,2048]{1,0:T(8,128)(2,1)} %all-gather.11.cloned.1.call-done, bf16[2048,1536]{1,0:T(8,128)(2,1)} %all-gather.13.cloned.1.call-done), kind=kOutput, calls=%fused_computation.116 | convolution fusion | flops 3240099840 | bytes 11565056 | tf_op jit(solution)/shard_map/dot_general | solution.py:203
  319.6 37.5 %all-gather.15.cloned.1.call-done = bf16[2048,1536]{1,0:T(8,128)(2,1)} async-done(((bf16[256,1536]{1,0:T(8,128)(2,1)}), bf16[2048,1536]{1,0:T(8,128)(2,1)}) %all-gather.15.cloned.1.call-update) | async-done | bytes 6291472 | tf_op jit(solution)/shard_map/all_gather | solution.py:206
  357.1 48.6 %all-gather.17.cloned.1.call-done = bf16[1536,2048]{1,0:T(8,128)(2,1)} async-done(((bf16[1536,256]{1,0:T(8,128)(2,1)}), bf16[1536,2048]{1,0:T(8,128)(2,1)}) %all-gather.17.cloned.1.call-update) | async-done | bytes 6291472 | tf_op jit(solution)/shard_map/all_gather | solution.py:210
  405.7 14.9 %fusion.46 = f32[515,2048]{1,0:T(8,128)} fusion(bf16[1536,2048]{1,0:T(8,128)(2,1)} %all-gather.17.cloned.1.call-done, bf16[515,2048]{1,0:T(8,128)(2,1)} %all-gather.11.cloned.1.call-done, bf16[2048,1536]{1,0:T(8,128)(2,1)} %all-gather.15.cloned.1.call-done, f32[515,1536]{1,0:T(8,128)} %fusion.90), kind=kOutput, calls=%fused_computation.48 | convolution fusion | flops 6484945920 | bytes 22075392 | tf_op jit(solution)/shard_map/dot_general | solution.py:208
  420.6 78.0 %reduce-scatter.5.cloned.1.call-done = f32[515,512]{1,0:T(8,128)} async-done(((f32[515,2048]{1,0:T(8,128)}), f32[515,512]{1,0:T(8,128)}) %reduce-scatter.5.cloned.1.call-update) | async-done | bytes 1054736 | tf_op jit(solution)/shard_map/reduce_scatter | solution.py:214
  498.6 1.5 add_convert_fusion
  500.1 0.8 slice.92
  500.9 0.6 slice.93
  (75 shorter events, 1.0 us)
Async XLA Ops:
  7.2 23.6 %copy-start.17 = (bf16[3,512]{1,0:T(4,128)(2,1)S(1)}, bf16[3,512]{1,0:T(4,128)(2,1)}, u32[]{:S(2)}) copy-start(bf16[3,512]{1,0:T(4,128)(2,1)} %param.20) | copy-start | bytes 9220
  7.2 31.9 %copy-start.19 = (s32[3]{0:T(128)S(1)}, s32[3]{0:T(128)}, u32[]{:S(2)}) copy-start(s32[3]{0:T(128)} %param.23) | copy-start | bytes 40
  7.2 32.6 %copy-start.11 = (bf16[512,2,256]{2,1,0:T(2,128)(2,1)S(1)}, bf16[512,2,256]{2,1,0:T(2,128)(2,1)}, u32[]{:S(2)}) copy-start(bf16[512,2,256]{2,1,0:T(2,128)(2,1)} %param.17) | copy-start | bytes 1572868
  7.2 124.1 %all-gather.9.cloned.1.call-start = ((), (), s32[]{:S(2)}) async-start(), calls=%async_computation.2 | async-start | bytes 2359296 | tf_op jit(solution)/shard_map/all_gather | solution.py:186
  7.9 206.8 %reduce-scatter.3.cloned.1.call-start = ((), (), s32[]{:S(2)}) async-start(), calls=%async_computation.3 | async-start | bytes 5324800 | tf_op jit(solution)/shard_map/reduce_scatter | solution.py:192
  42.2 3.6 copy-start.1
  42.2 2.2 copy-start.10
  48.6 3.0 copy-start.8
  48.8 4.3 copy-start.12
  48.8 5.6 %copy-start.18 = (bf16[3,2,256]{2,1,0:T(2,128)(2,1)S(1)}, bf16[3,2,256]{2,1,0:T(2,128)(2,1)}, u32[]{:S(2)}) copy-start(bf16[3,2,256]{2,1,0:T(2,128)(2,1)} %param.21) | copy-start | bytes 9220
  84.0 3.4 copy-start.9
  87.3 8.9 %copy-start.20 = (s32[3]{0:T(128)S(1)}, s32[3]{0:T(128)}, u32[]{:S(2)}) copy-start(s32[3]{0:T(128)} %param.24) | copy-start | bytes 40
  87.3 12.6 %copy-start.13 = (f32[512,2,64]{2,0,1:T(8,128)S(1)}, f32[512,2,64]{2,0,1:T(8,128)}, u32[]{:S(2)}) copy-start(f32[512,2,64]{2,0,1:T(8,128)} %get-tuple-element.28) | copy-start | bytes 786436
  87.9 12.0 %copy-start.2 = (f32[512,2,128]{2,0,1:T(8,128)S(1)}, f32[512,2,128]{2,0,1:T(8,128)}, u32[]{:S(2)}) copy-start(f32[512,2,128]{2,0,1:T(8,128)} %copy-done.1) | copy-start | bytes 1572868
  87.9 13.3 %copy-start.4 = (f32[512,2,2,128]{3,2,1,0:T(2,128)S(1)}, f32[512,2,2,128]{3,2,1,0:T(2,128)}, u32[]{:S(2)}) copy-start(f32[512,2,2,128]{3,2,1,0:T(2,128)} %reshape.328) | copy-start | bytes 3145732
  87.9 13.3 %copy-start.5 = (bf16[2048,2,128]{2,0,1:T(8,128)(2,1)S(1)}, bf16[2048,2,128]{2,0,1:T(8,128)(2,1)}, u32[]{:S(2)}) copy-start(bf16[2048,2,128]{2,0,1:T(8,128)(2,1)} %copy.64) | copy-start | bytes 3145732
  96.6 4.6 copy-start.6
  96.7 4.6 copy-start.7
  111.3 9.6 %copy-start.14 = (bf16[1,1,2048,256]{2,3,1,0:T(8,128)(2,1)S(1)}, bf16[1,1,2048,256]{2,3,1,0:T(8,128)(2,1)}, u32[]{:S(2)}) copy-start(bf16[1,1,2048,256]{2,3,1,0:T(8,128)(2,1)} %copy.57) | copy-start | bytes 3145732
  111.3 9.6 %copy-start.15 = (bf16[512,1,256]{0,2,1:T(8,128)(2,1)S(1)}, bf16[512,1,256]{0,2,1:T(8,128)(2,1)}, u32[]{:S(2)}) copy-start(bf16[512,1,256]{0,2,1:T(8,128)(2,1)} %copy.58) | copy-start | bytes 786436
  136.3 78.4 %copy-start.3 = (bf16[512,512]{1,0:T(8,128)(2,1)S(1)}, bf16[512,512]{1,0:T(8,128)(2,1)}, u32[]{:S(2)}) copy-start(bf16[512,512]{1,0:T(8,128)(2,1)} %param.25) | copy-start | bytes 1572868
  136.3 78.4 %copy-start.16 = (bf16[3,512]{1,0:T(4,128)(2,1)S(1)}, bf16[3,512]{1,0:T(4,128)(2,1)}, u32[]{:S(2)}) copy-start(bf16[3,512]{1,0:T(4,128)(2,1)} %param.26) | copy-start | bytes 9220
  136.3 126.5 %all-gather.13.cloned.1.call-start = ((), (), s32[]{:S(2)}) async-start(), calls=%async_computation.5 | async-start | bytes 7077888 | tf_op jit(solution)/shard_map/all_gather | solution.py:205
  137.0 173.9 %all-gather.11.cloned.1.call-start = ((), (), s32[]{:S(2)}) async-start(), calls=%async_computation.4 | async-start | bytes 2662400 | tf_op jit(solution)/shard_map/all_gather | solution.py:200
  229.4 127.8 %all-gather.15.cloned.1.call-start = ((), (), s32[]{:S(2)}) async-start(), calls=%async_computation.6 | async-start | bytes 7077888 | tf_op jit(solution)/shard_map/all_gather | solution.py:206
  230.0 175.8 %all-gather.17.cloned.1.call-start = ((), (), s32[]{:S(2)}) async-start(), calls=%async_computation.7 | async-start | bytes 7077888 | tf_op jit(solution)/shard_map/all_gather | solution.py:210
  230.5 268.1 %reduce-scatter.5.cloned.1.call-start = ((), (), s32[]{:S(2)}) async-start(), calls=%async_computation.8 | async-start | bytes 5324800 | tf_op jit(solution)/shard_map/reduce_scatter | solution.py:214
  420.6 78.0 %copy-start = (f32[515,512]{1,0:T(8,128)S(1)}, f32[515,512]{1,0:T(8,128)}, u32[]{:S(2)}) copy-start(f32[515,512]{1,0:T(8,128)} %reduce-scatter.3.cloned.1.call-done) | copy-start | bytes 3164164
Sparse Core Ops, SparseCore 0:
  9.9 31.0 all-gather.8
  136.4 78.2 reduce-scatter.2
  216.7 46.0 all-gather.12
  264.3 46.5 all-gather.10
  312.8 44.2 all-gather.14
  359.0 46.6 all-gather.16
  420.7 77.7 reduce-scatter.4
where the time goes:
time: 509 us; the launch traced here: 508 us
  waiting for transfers between devices  324 us (64%)
  matrix products  53.1 us (10%)
  blocking collectives  51.8 us (10%)
  local copies, waits for them, and re-layouts  38.3 us (8%)
  other arithmetic  25.3 us (5%)
  between operations  15.8 us (3%)
    reduce_scatter x1, waiting for transfers between devices, body(): lax.psum_scatter(down_terms, 'head', scatter_dimension=1, tiled=True)  78 us
    reduce_scatter x1, waiting for transfers between devices, body(): lax.psum_scatter(partial_value, 'head', scatter_dimension=1, tiled=True)  76.8 us
    all_gather x1, waiting for transfers between devices, body(): lax.all_gather(down_weight, 'req', axis=1, tiled=True)  48.6 us
    all_gather x1, waiting for transfers between devices, body(): normed = lax.all_gather(normed_share, 'head', axis=1, tiled=True)  48.1 us
    all_gather x1, waiting for transfers between devices, body(): upper = add_rows(lax.all_gather(up_weight, 'req', axis=0, tiled=True))  37.5 us
    all_gather x1, waiting for transfers between devices, body(): gate_sum = add_rows(lax.all_gather(gate_weight, 'req', axis=0, tiled=True))  32 us
    unnamed x1, blocking collectives  15.3 us
    dot_general x1, matrix products, body(): jnp.dot(hidden, lax.all_gather(down_weight, 'req', axis=1, tiled=True), p...  14.9 us
  transfers between devices with their start and end apart: 7, of which 6 were waited for; matrix products, arithmetic and copies ran while one was open for 18% of the time, Pallas kernels for 0%

commit v1 on v0

--- a/solution.py
+++ b/solution.py
@@ -1,8 +1,11 @@
+import functools
 import math
 
 import jax
 import jax.numpy as jnp
 from jax import lax
+from jax.experimental import pallas as pl
+from jax.experimental.pallas import tpu as pltpu
 from jax.sharding import PartitionSpec as P
 
 HEAD_SIZE = 128
@@ -217,6 +220,577 @@
     return (result[:prefill_rows], result[prefill_rows:])
 
 
+MESH = pl.DeviceIdType.MESH
+BF = jnp.bfloat16
+F32 = jnp.float32
+CHUNKS = 3
+PAD = 16
+
+
+def mm(a, b):
+    return jnp.dot(a, b, preferred_element_type=F32)
+
+
+def mm_t(a, b):
+    return lax.dot_general(a, b, (((1,), (1,)), ((), ())), preferred_element_type=F32)
+
+
+def turn(x, cosine, signed_sine):
+    return x * cosine + pltpu.roll(x, 64, 1) * signed_sine
+
+
+class Gather:
+    def __init__(self, me, shard, slot_of, send, recv, own):
+        self.me = me
+        self.sib = me + 1 - 2 * (me % 2)
+        self.xn = me + 2 - 4 * ((me // 2) % 2)
+        self.yn = me + 4 - 8 * (me // 4)
+        self.dg = self.yn + 2 - 4 * ((me // 2) % 2)
+        self.half = shard.shape[0] // 2
+        self.shard, self.slot, self.send, self.recv, self.own = shard, slot_of, send, recv, own
+
+    def copy(self, at, src, dst, to):
+        return pltpu.make_async_remote_copy(
+            src_ref=src,
+            dst_ref=dst,
+            send_sem=self.send.at[at],
+            recv_sem=self.recv.at[at],
+            device_id={"req": to},
+            device_id_type=MESH,
+        )
+
+    def part(self, who, k):
+        return self.slot(who).at[pl.ds(k * self.half, self.half)]
+
+    def copies(self):
+        mine = self.slot(self.me)
+        sx, sy = self.slot(self.xn), self.slot(self.yn)
+        d0, d1 = self.part(self.dg, 0), self.part(self.dg, 1)
+        x0, y1 = self.part(self.xn, 0), self.part(self.yn, 1)
+        return [
+            self.copy(0, self.shard, mine, self.xn),
+            self.copy(1, self.shard, mine, self.yn),
+            self.copy(2, self.shard, mine, self.sib),
+            self.copy(3, x0, x0, self.yn),
+            self.copy(4, sx, sx, self.sib),
+            self.copy(5, y1, y1, self.xn),
+            self.copy(6, sy, sy, self.sib),
+            self.copy(7, d0, d0, self.sib),
+            self.copy(8, d1, d1, self.sib),
+        ]
+
+    def begin(self):
+        self.all = self.copies()
+        for at in (0, 1, 2):
+            self.all[at].start()
+        self.local = pltpu.make_async_copy(self.shard, self.slot(self.me), self.own)
+        self.local.start()
+
+    def middle(self):
+        self.all[0].wait_recv()
+        self.all[3].start()
+        self.all[4].start()
+        self.all[1].wait_recv()
+        self.all[5].start()
+        self.all[6].start()
+
+    def last(self):
+        self.all[3].wait_recv()
+        self.all[7].start()
+        self.all[5].wait_recv()
+        self.all[8].start()
+
+    def finish(self):
+        for at in (2, 4, 6, 7, 8):
+            self.all[at].wait_recv()
+        for one in self.all:
+            one.wait_send()
+        self.local.wait()
+
+
+def attention_kernel(
+    n, slots,
+    q_ref, fk_ref, fv_ref, pc_ref, cos_ref, sin_ref, start_ref,
+    tok_ref, dcos_ref, dsin_ref, dlen_ref, rid_ref, dc_ref, proj_ref, gate_ref,
+    att_ref, projg_ref, gateg_ref,
+    kbuf, vbuf, dbuf, toks, atts, myatt, qrot,
+    local_sem, tok_send, tok_recv, att_send, att_recv, w_send, w_recv,
+):
+    me = lax.axis_index("req")
+    cache = pc_ref.shape[1]
+    span = q_ref.shape[0]
+    loads = [
+        pltpu.make_async_copy(dc_ref, dbuf, local_sem.at[0]),
+        pltpu.make_async_copy(pc_ref.at[0], kbuf.at[pl.ds(0, cache)], local_sem.at[1]),
+        pltpu.make_async_copy(pc_ref.at[1], vbuf.at[pl.ds(0, cache)], local_sem.at[2]),
+    ]
+    for one in loads:
+        one.start()
+    barrier = pltpu.get_barrier_semaphore()
+    for j in range(1, n):
+        pl.semaphore_signal(
+            barrier, inc=1, device_id={"req": (me + j) % n}, device_id_type=MESH
+        )
+    pl.semaphore_wait(barrier, n - 1)
+
+    def spread(src, dst, send, recv):
+        return [
+            pltpu.make_async_remote_copy(
+                src_ref=src,
+                dst_ref=dst.at[me],
+                send_sem=send.at[j],
+                recv_sem=recv.at[j],
+                device_id={"req": (me + j) % n},
+                device_id_type=MESH,
+            )
+            for j in range(1, n)
+        ]
+
+    tok_copies = spread(tok_ref, toks, tok_send, tok_recv)
+    for one in tok_copies:
+        one.start()
+    rows_of = gate_ref.shape[0]
+    first = Gather(
+        me, proj_ref, lambda who: projg_ref.at[who], w_send.at[0], w_recv.at[0], local_sem.at[3]
+    )
+    second = Gather(
+        me, gate_ref, lambda who: gateg_ref.at[pl.ds(who * rows_of, rows_of)],
+        w_send.at[1], w_recv.at[1], local_sem.at[4],
+    )
+    first.begin()
+    second.begin()
+    toks[me] = tok_ref[...]
+
+    factor = 1.4426950408889634 / math.sqrt(HEAD_SIZE)
+    for h in range(4):
+        at = pl.ds(h * 128, 128)
+        qrot[:, at] = turn(q_ref[:, at].astype(F32), cos_ref[...], sin_ref[...]).astype(BF)
+    for one in loads:
+        one.wait()
+    for g in range(2):
+        at = pl.ds(g * 128, 128)
+        kbuf[pl.ds(cache, span), at] = turn(
+            fk_ref[:, at].astype(F32), cos_ref[...], sin_ref[...]
+        ).astype(BF)
+    vbuf[pl.ds(cache, span), :] = fv_ref[...]
+
+    for one in tok_copies:
+        one.wait_recv()
+    tokens = toks[...].reshape(n * PAD, toks.shape[2])
+    marks = tokens[:, 1024:1152].astype(F32)
+    lane = lax.broadcasted_iota(jnp.int32, marks.shape, 1)
+    wanted = jnp.where(lane < slots, me * slots + lane, -7).astype(F32)
+    picker = jnp.where(marks == wanted, 1.0, 0.0).T[:PAD].astype(BF)
+    own = mm(picker, tokens[:, :1024])[:8]
+    dcos, dsin = dcos_ref[...], dsin_ref[...]
+    row16 = lax.broadcasted_iota(jnp.int32, (16, 1), 0) % 8
+    col = lax.broadcasted_iota(jnp.int32, (16, cache), 1)
+    seen = col < dlen_ref[:, 0:1]
+    for g in range(2):
+        heads = [
+            turn(own[:, (2 * g + j) * 128:(2 * g + j + 1) * 128], dcos, dsin) for j in range(2)
+        ]
+        query = jnp.concatenate(heads, axis=0).astype(BF)
+        key = turn(own[:, 512 + g * 128:512 + (g + 1) * 128], dcos, dsin).astype(BF).astype(F32)
+        value = own[:, 768 + g * 128:768 + (g + 1) * 128]
+        at = pl.ds(g * 128, 128)
+        scores = jnp.zeros((16, cache), F32)
+        for s in range(slots):
+            scores = jnp.where(row16 == s, mm_t(query, dbuf[s, 0, :, at]), scores)
+        scores = jnp.where(seen, scores, -1e30)
+        new = jnp.sum(
+            query.astype(F32) * jnp.concatenate([key, key], axis=0), axis=1, keepdims=True
+        )
+        top = jnp.maximum(jnp.max(scores, axis=1, keepdims=True), new)
+        raw = jnp.exp2((scores - top) * factor)
+        raw_new = jnp.exp2((new - top) * factor)
+        totals = jnp.sum(raw, axis=1, keepdims=True) + raw_new
+        raw16 = raw.astype(BF)
+        mixed = jnp.zeros((16, 128), F32)
+        for s in range(slots):
+            mixed = jnp.where(row16 == s, mm(raw16, dbuf[s, 1, :, at]), mixed)
+        mixed = mixed + raw_new.astype(BF).astype(F32) * jnp.concatenate([value, value], axis=0)
+        mixed = mixed / totals
+        for j in range(2):
+            piece = jnp.concatenate([mixed[j * 8:j * 8 + 8], jnp.zeros((8, 128), F32)], axis=0)
+            myatt[:, pl.ds((2 * g + j) * 128, 128)] = piece.astype(BF)
+    att_copies = spread(myatt, atts, att_send, att_recv)
+    for one in att_copies:
+        one.start()
+    atts[me] = myatt[...]
+    first.middle()
+
+    start = start_ref[0:1, 0:1]
+    bias = jnp.where(lax.broadcasted_iota(jnp.int32, (1, cache), 1) < start, 0.0, -1e30)
+    block = 128
+    for g in range(2):
+        at = pl.ds(g * 128, 128)
+
+        def one_block(i, carry, g=g, at=at):
+            rows = pl.ds(pl.multiple_of(i * block, block), block)
+            query = jnp.concatenate(
+                [qrot[rows, pl.ds((2 * g + j) * 128, 128)] for j in range(2)], axis=0
+            )
+            old = mm_t(query, kbuf[pl.ds(0, cache), at]) + bias
+            new = mm_t(query, kbuf[pl.ds(cache, span), at])
+            row = lax.broadcasted_iota(jnp.int32, new.shape, 0) % block + i * block
+            new = jnp.where(lax.broadcasted_iota(jnp.int32, new.shape, 1) <= row, new, -1e30)
+            top = jnp.maximum(
+                jnp.max(old, axis=1, keepdims=True), jnp.max(new, axis=1, keepdims=True)
+            )
+            raw_old = jnp.exp2((old - top) * factor)
+            raw_new = jnp.exp2((new - top) * factor)
+            totals = jnp.sum(raw_old, axis=1, keepdims=True) + jnp.sum(
+                raw_new, axis=1, keepdims=True
+            )
+            mixed = mm(raw_old.astype(BF), vbuf[pl.ds(0, cache), at]) + mm(
+                raw_new.astype(BF), vbuf[pl.ds(cache, span), at]
+            )
+            mixed = (mixed / totals).astype(BF)
+            for j in range(2):
+                att_ref[rows, pl.ds((2 * g + j) * 128, 128)] = mixed[j * block:(j + 1) * block]
+            return carry
+
+        lax.fori_loop(0, span // block, one_block, 0)
+        if g == 0:
+            second.middle()
+            first.last()
+    for one in att_copies:
+        one.wait_recv()
+    every = atts[...].reshape(n * PAD, atts.shape[2])
+    pick = lax.broadcasted_iota(jnp.int32, (PAD, n * PAD), 1) == rid_ref[:, 0:1]
+    att_ref[pl.ds(span, PAD), :] = mm(jnp.where(pick, 1.0, 0.0).astype(BF), every).astype(BF)
+    second.last()
+    first.finish()
+    second.finish()
+    for one in tok_copies + att_copies:
+        one.wait_send()
+
+
+def layer_kernel(
+    heads,
+    att_ref, st_ref, projg_ref, gain_ref, gateg_ref, up_ref, down_ref,
+    res_ref,
+    terms, summed, gath, hidden, gate_v, up_v, down_v,
+    up1, dn1, up1s, dn1s, up2, dn2, up2s, dn2s,
+    local_sem, w_send, w_recv, rs_send, rs_recv, ag_send, ag_recv,
+):
+    me = lax.axis_index("req")
+    z = lax.axis_index("head")
+    top = heads - 1
+    rows = gath.shape[2]
+    share = gath.shape[3]
+    width = heads * share
+    rows_of = up_ref.shape[0]
+    gate_load = pltpu.make_async_copy(gateg_ref, gate_v, local_sem.at[2])
+    gate_load.start()
+    gu = Gather(
+        me, up_ref, lambda who: up_v.at[pl.ds(who * rows_of, rows_of)],
+        w_send.at[0], w_recv.at[0], local_sem.at[0],
+    )
+    gd = Gather(
+        me, down_ref, lambda who: down_v.at[who], w_send.at[1], w_recv.at[1], local_sem.at[1]
+    )
+    barrier = pltpu.get_barrier_semaphore()
+    for other in (gu.sib, gu.xn, gu.yn):
+        pl.semaphore_signal(barrier, inc=1, device_id={"req": other}, device_id_type=MESH)
+
+    @pl.when(z > 0)
+    def _():
+        pl.semaphore_signal(barrier, inc=1, device_id={"head": z - 1}, device_id_type=MESH)
+
+    @pl.when(z < top)
+    def _():
+        pl.semaphore_signal(barrier, inc=1, device_id={"head": z + 1}, device_id_type=MESH)
+
+    pl.semaphore_wait(
+        barrier, 3 + (z > 0).astype(jnp.int32) + (z < top).astype(jnp.int32)
+    )
+
+    gu.begin()
+    gd.begin()
+
+    def line_copy(src, dst, send, recv, step):
+        return pltpu.make_async_remote_copy(
+            src_ref=src, dst_ref=dst, send_sem=send, recv_sem=recv,
+            device_id={"head": z + step}, device_id_type=MESH,
+        )
+
+    class Sums:
+        def __init__(self, phase, ups, dns, ups_out, dns_out):
+            self.phase = phase
+            self.bufs = {1: (ups_out, ups), -1: (dns_out, dns)}
+
+        def copy(self, step, d, c):
+            out, into = self.bufs[step]
+            at = (self.phase, (1 - step) // 2, d, c)
+            return line_copy(
+                out.at[d, c], into.at[d, c], rs_send.at[at], rs_recv.at[at], step
+            )
+
+        def send(self, c):
+            for k in range(heads - 1):
+                for step, d in ((1, top - k), (-1, k)):
+                    out, into = self.bufs[step]
+                    goes = z < d if step == 1 else z > d
+                    ends = z == 0 if step == 1 else z == top
+
+                    @pl.when(jnp.logical_and(goes, ends))
+                    def _():
+                        out[d, c] = terms[d, c].astype(BF)
+                        self.copy(step, d, c).start()
+
+                    @pl.when(jnp.logical_and(goes, jnp.logical_not(ends)))
+                    def _():
+                        self.copy(step, d, c).wait_recv()
+                        out[d, c] = (terms[d, c] + into[d, c].astype(F32)).astype(BF)
+                        self.copy(step, d, c).start()
+
+        def total(self, c, base):
+            summed[c] = terms[z, c] + base
+            for step in (1, -1):
+                into = self.bufs[step][1]
+                ends = z == 0 if step == 1 else z == top
+                for d in range(heads):
+
+                    @pl.when(jnp.logical_and(z == d, jnp.logical_not(ends)))
+                    def _():
+                        self.copy(step, d, c).wait_recv()
+                        summed[c] = summed[c] + into[d, c].astype(F32)
+
+        def finish(self):
+            for step in (1, -1):
+                for d in range(heads):
+
+                    @pl.when(z < d if step == 1 else z > d)
+                    def _():
+                        for c in range(CHUNKS):
+                            self.copy(step, d, c).wait_send()
+
+    def ag_copy(step, hop, c):
+        src = gath.at[z - step * (hop - 1), c]
+        at = ((1 - step) // 2, hop - 1, c)
+        return line_copy(src, src, ag_send.at[at], ag_recv.at[at], step)
+
+    def ag_wait(step, hop, c):
+        src = gath.at[z - step * hop, c]
+        at = ((1 - step) // 2, hop - 1, c)
+        line_copy(src, src, ag_send.at[at], ag_recv.at[at], -step).wait_recv()
+
+    def sends(step, hop):
+        if step == 1:
+            return jnp.logical_and(z < top, z - (hop - 1) >= 0)
+        return jnp.logical_and(z > 0, z + (hop - 1) <= top)
+
+    def receives(step, hop):
+        return z - hop >= 0 if step == 1 else z + hop <= top
+
+    def ag_own(c):
+        gath[z, c] = (summed[c] * gain_ref[z]).astype(BF)
+        for step in (1, -1):
+
+            @pl.when(sends(step, 1))
+            def _():
+                ag_copy(step, 1, c).start()
+
+    def ag_forward(c):
+        for hop in range(1, heads):
+            for step in (1, -1):
+
+                @pl.when(receives(step, hop))
+                def _():
+                    ag_wait(step, hop, c)
+
+                if hop < heads - 1:
+
+                    @pl.when(sends(step, hop + 1))
+                    def _():
+                        ag_copy(step, hop + 1, c).start()
+
+    def ag_finish():
+        for hop in range(1, heads):
+            for step in (1, -1):
+
+                @pl.when(sends(step, hop))
+                def _():
+                    for c in range(CHUNKS):
+                        ag_copy(step, hop, c).wait_send()
+
+    def base(c):
+        return st_ref[pl.ds(c * rows, rows), :].astype(F32)
+
+    def project(c):
+        for b in range(projg_ref.shape[0]):
+            terms[b // 2, c, :, pl.ds((b % 2) * 256, 256)] = mm(
+                att_ref[pl.ds(c * rows, rows), :], projg_ref[b]
+            )
+
+    def feed(c):
+        squares = jnp.zeros((rows, 1), F32)
+        for o in range(heads):
+            plain = gath[o, c].astype(F32) / gain_ref[o]
+            squares = squares + jnp.sum(plain * plain, axis=1, keepdims=True)
+        scale = lax.rsqrt(squares / width + norm_eps)
+
+        def tile(t, carry):
+            at = pl.ds(pl.multiple_of(t * 256, 256), 256)
+            gate = jnp.zeros((rows, 256), F32)
+            up = jnp.zeros((rows, 256), F32)
+            for o in range(heads):
+                u = gath[o, c]
+                gate = gate + mm(u, gate_v[pl.ds(o * share, share), at])
+                up = up + mm(u, up_v[pl.ds(o * share, share), at])
+            gate = gate * scale
+            hidden[:, at] = (gate / (1.0 + jnp.exp(-gate)) * (up * scale)).astype(BF)
+            return carry
+
+        lax.fori_loop(0, hidden.shape[1] // 256, tile, 0)
+        for b in range(down_v.shape[0]):
+            terms[b // 2, c, :, pl.ds((b % 2) * 256, 256)] = mm(hidden[...], down_v[b])
+
+    one = Sums(0, up1, dn1, up1s, dn1s)
+    two = Sums(1, up2, dn2, up2s, dn2s)
+    project(0)
+    one.send(0)
+    project(1)
+    one.send(1)
+    project(2)
+    one.total(0, base(0))
+    ag_own(0)
+    one.send(2)
+    gu.middle()
+    one.total(1, base(1))
+    ag_own(1)
+    ag_forward(0)
+    one.total(2, base(2))
+    ag_own(2)
+    gd.middle()
+    gu.last()
+    ag_forward(1)
+    ag_forward(2)
+    gd.last()
+    gate_load.wait()
+    gu.finish()
+    gd.finish()
+    feed(0)
+    two.send(0)
+    feed(1)
+    two.send(1)
+    feed(2)
+    two.total(0, summed[0])
+    two.send(2)
+    two.total(1, summed[1])
+    two.total(2, summed[2])
+    for c in range(CHUNKS):
+        res_ref[pl.ds(c * rows, rows), :] = summed[c].astype(BF)
+    one.finish()
+    two.finish()
+    ag_finish()
+
+
+def padded(array, rows, fill=0):
+    return jnp.pad(array, ((0, rows - array.shape[0]), (0, 0)), constant_values=fill)
+
+
+def signed_tables(positions):
+    cosine, sine = rope_tables(positions, HEAD_SIZE)
+    half = HEAD_SIZE // 2
+    return cosine, jnp.concatenate([-sine[:, :half], sine[:, half:]], axis=1)
+
+
+def fast_body(
+    prefill_query, prefill_new_pairs, prefill_cache, prefill_start, decode_query, decode_fresh,
+    decode_cache, decode_length, decode_slot, prefill_states, decode_states, output_proj,
+    norm_gain, gate_weight, up_weight, down_weight,
+):
+    n = lax.axis_size("req")
+    heads = lax.axis_size("head")
+    span, share = prefill_query.shape
+    slots = decode_query.shape[0]
+    rows = span + PAD
+    cosine, sine = signed_tables(prefill_start[0] + jnp.arange(span, dtype=jnp.int32))
+    dcos, dsin = signed_tables(jnp.pad(decode_length, (0, 8 - slots)))
+    start = jnp.broadcast_to(prefill_start[:, None], (8, 128))
+    lens = jnp.pad(decode_length, (0, 8 - slots), constant_values=1)
+    dlen = jnp.broadcast_to(jnp.concatenate([lens, lens])[:, None], (16, 128))
+    rid = (decode_slot // slots) * PAD + decode_slot % slots
+    rid = jnp.broadcast_to(jnp.pad(rid, (0, PAD - slots), constant_values=-1)[:, None], (PAD, 128))
+    marks = jnp.broadcast_to(
+        jnp.pad(decode_slot, (0, PAD - slots), constant_values=-1)[:, None], (PAD, 128)
+    ).astype(BF)
+    token = jnp.concatenate(
+        [padded(decode_query, PAD), padded(decode_fresh.reshape(slots, -1), PAD), marks], axis=1
+    )
+    vm = pl.BlockSpec(memory_space=pltpu.VMEM)
+    hbm = pl.BlockSpec(memory_space=pl.ANY)
+    dma = pltpu.SemaphoreType.DMA
+    cache = prefill_cache.shape[2]
+    kv = prefill_cache.shape[3]
+    ff = gate_weight.shape[1]
+    att, projg, gateg = pl.pallas_call(
+        functools.partial(attention_kernel, n, slots),
+        out_shape=[
+            jax.ShapeDtypeStruct((rows, share), BF),
+            jax.ShapeDtypeStruct((n,) + output_proj.shape, BF),
+            jax.ShapeDtypeStruct((n * gate_weight.shape[0], ff), BF),
+        ],
+        in_specs=[vm, vm, vm, hbm, vm, vm, vm, vm, vm, vm, vm, vm, hbm, hbm, hbm],
+        out_specs=[vm, hbm, hbm],
+        scratch_shapes=[
+            pltpu.VMEM((cache + span, kv), BF),
+            pltpu.VMEM((cache + span, kv), BF),
+            pltpu.VMEM(decode_cache.shape, BF),
+            pltpu.VMEM((n, PAD, token.shape[1]), BF),
+            pltpu.VMEM((n, PAD, share), BF),
+            pltpu.VMEM((PAD, share), BF),
+            pltpu.VMEM((span, share), BF),
+            dma((5,)), dma((n,)), dma((n,)), dma((n,)), dma((n,)), dma((2, 9)), dma((2, 9)),
+        ],
+        compiler_params=pltpu.CompilerParams(
+            collective_id=0, has_side_effects=True, vmem_limit_bytes=48 * 2**20
+        ),
+        cost_estimate=pl.CostEstimate(
+            flops=3 * 10**9, bytes_accessed=30 * 10**6, transcendentals=6 * 10**6
+        ),
+        name="attend_and_gather",
+    )(
+        prefill_query, prefill_new_pairs[:, 0], prefill_new_pairs[:, 1], prefill_cache[0],
+        cosine, sine, start, token, dcos, dsin, dlen, rid, decode_cache, output_proj, gate_weight,
+    )
+    states = jnp.concatenate([prefill_states, padded(decode_states, PAD)], axis=0)
+    gain = norm_gain.astype(F32).reshape(heads, 1, share)
+    line = (heads, CHUNKS, rows // CHUNKS, share)
+    result = pl.pallas_call(
+        functools.partial(layer_kernel, heads),
+        out_shape=jax.ShapeDtypeStruct((rows, share), BF),
+        in_specs=[vm, vm, vm, vm, hbm, hbm, hbm],
+        out_specs=vm,
+        scratch_shapes=[
+            pltpu.VMEM(line, F32),
+            pltpu.VMEM(line[1:], F32),
+            pltpu.VMEM(line, BF),
+            pltpu.VMEM((rows // CHUNKS, ff), BF),
+            pltpu.VMEM(gateg.shape, BF),
+            pltpu.VMEM(gateg.shape, BF),
+            pltpu.VMEM((n,) + down_weight.shape, BF),
+        ]
+        + [pltpu.VMEM(line, BF)] * 8
+        + [
+            dma((3,)), dma((2, 9)), dma((2, 9)),
+            dma((2, 2, heads, CHUNKS)), dma((2, 2, heads, CHUNKS)),
+            dma((2, heads - 1, CHUNKS)), dma((2, heads - 1, CHUNKS)),
+        ],
+        compiler_params=pltpu.CompilerParams(
+            collective_id=1, has_side_effects=True, vmem_limit_bytes=60 * 2**20
+        ),
+        cost_estimate=pl.CostEstimate(
+            flops=11 * 10**9, bytes_accessed=40 * 10**6, transcendentals=10**6
+        ),
+        name="project_and_feed",
+    )(att, states, projg, gain, gateg, up_weight, down_weight)
+    return result[:span], result[span:span + slots]
+
+
 def solution(mesh):
     in_specs = (
         P("req", "head"),
@@ -237,4 +811,6 @@
         P("head", "req"),
     )
     out_specs = (P("req", "head"), P("req", "head"))
-    return jax.shard_map(body, mesh=mesh, in_specs=in_specs, out_specs=out_specs, check_vma=False)
+    fits = mesh.shape["req"] == 8
+    return jax.shard_map(
+        fast_body if fits else body, mesh=mesh, in_specs=in_specs, out_specs=out_specs, check_vma=False)

time: 509 us -> 203 us (0.40)
  waiting for transfers between devices: 324 us -> 0 us
  Pallas kernels: 0 us -> 191 us
  matrix products: 53.1 us -> 0 us
  blocking collectives: 51.8 us -> 0 us
  local copies, waits for them, and re-layouts: 38.3 us -> 7.36 us
  other arithmetic: 25.3 us -> 2.94 us
  between operations: 15.8 us -> 1.46 us
    pallas_call x0 -> x2, Pallas kernels: none -> 191 us  [the longest x1 145 us: fast_body(): pl.pallas_call(functools.partial(layer_kernel, heads), out_shape=jax.Shap...]
    all_gather x5 -> x0, waiting for transfers between devices: 166 us -> none  [the longest x1 48.6 us: body(): lax.all_gather(down_weight, 'req', axis=1, tiled=True)]
    reduce_scatter x2 -> x0, waiting for transfers between devices: 155 us -> none  [the longest x1 78 us: body(): lax.psum_scatter(down_terms, 'head', scatter_dimension=1, tiled=True)]
    dot_general x10 -> x0, matrix products: 53.1 us -> none  [the longest x1 14.9 us: body(): jnp.dot(hidden, lax.all_gather(down_weight, 'req', axis=1, tiled=True), p...]
    all_gather x3 -> x0, blocking collectives: 25.5 us -> none  [the longest x1 9.28 us: body(): lax.all_gather(fresh_flat, 'req', axis=0, tiled=True)]
    unnamed x1 -> x0, blocking collectives: 15.3 us -> none
    reduce_sum x3 -> x0, other arithmetic: 11.3 us -> none  [the longest x2 9.86 us: attend(): totals = jnp.sum(unnormed, axis=-1, keepdims=True)]
    psum x1 -> x0, blocking collectives: 10.9 us -> none  [body(): squares = lax.psum(jnp.sum(summed * summed, axis=1), 'head')]
  transfers between devices with their start and end apart: 7 -> 0, of which waited for: 6 -> 0; matrix products, arithmetic and copies ran while one was open for 18% -> 0% of each run, Pallas kernels for 0% -> 0%
where the time goes in v1:
time: 203 us
  Pallas kernels  191 us (94%)
  local copies, waits for them, and re-layouts  7.36 us (4%)
  other arithmetic  2.94 us (1%)
    pallas_call x1, Pallas kernels, fast_body(): pl.pallas_call(functools.partial(layer_kernel, heads), out_shape=jax.Shap...  145 us
    pallas_call x1, Pallas kernels, fast_body(): pl.pallas_call(functools.partial(attention_kernel, n, slots), out_shape=[...  46.8 us

profile of v1, /device:TPU:0, one launch (start us, length us, event | category | flops | bytes accessed | tf_op | source)
XLA Modules:
  0.0 203.1 jit_solution(4611786473582423609)
XLA Ops:
  0.6 0.0 copy-start.11
  1.3 0.0 copy-start.5
  1.3 1.0 fusion.2
  2.3 0.2 pad_maximum_fusion
  2.5 0.0 copy-done.11
  2.6 0.1 fusion.8
  2.7 0.1 pad_maximum_fusion.2
  2.8 0.0 copy-done.5
  2.8 0.7 fusion.10
  3.5 0.0 copy-start.12
  3.5 0.0 copy-start.10
  3.5 0.0 copy-start.8
  3.5 0.0 copy-start
  3.5 0.0 copy-start.1
  3.6 0.0 copy-start.2
  3.6 0.1 copy_bitcast_fusion
  3.7 0.5 copy-done.12
  4.2 0.1 broadcast_in_dim.9
  4.3 0.0 copy-done.10
  4.3 0.0 copy-done.8
  4.3 0.1 pad_add_fusion
  4.4 0.1 broadcast_in_dim.10.dlen_ref
  4.4 0.1 broadcast_in_dim.11.rid_ref
  4.5 0.2 copy-done
  4.7 0.1 copy-done.1
  4.8 0.1 copy-done.2
  4.9 0.0 copy-start.6
  4.9 0.0 copy-start.7
  4.9 0.0 copy-start.9
  4.9 46.8 %attend_and_gather.1 = (bf16[528,512]{1,0:T(8,128)(2,1)S(1)}, bf16[8,512,256]{2,1,0:T(8,128)(2,1)S(1)}, bf16[2048,1536]{1,0:T(8,128)(2,1)}) custom-call(bf16[512,512]{1,0:T(8,128)(2,1)S(1)} %copy-done.1, bf16[512,256]{1,0:T(8,128)(2,1)S(1)} %get-tuple-element.21.fk_ref, bf16[512,256]{1,0:T(8,128)(2,1)S(1)} %get-tuple-element.20.fv_ref, ...), custom_call_target="tpu_custom_call" | custom-call | flops 3000000000 | bytes 30000000 | tf_op jit(solution)/shard_map/attend_and_gather/pallas_call | solution.py:730
  51.7 0.0 copy-start.3
  51.7 1.4 copy-done.3
  53.0 0.0 copy-start.4
  53.0 0.9 copy-done.4
  53.9 0.0 copy-done.6
  53.9 0.0 copy-done.7
  53.9 0.8 fusion.1.st_ref
  54.7 0.0 copy-done.9
  54.7 0.6 reshape.30
  55.3 144.6 %project_and_feed.1 = bf16[528,512]{1,0:T(8,128)(2,1)} custom-call(bf16[528,512]{1,0:T(8,128)(2,1)} %copy-done.4, bf16[528,512]{1,0:T(8,128)(2,1)} %fusion.1.st_ref, bf16[8,512,256]{2,1,0:T(8,128)(2,1)} %copy-done.3, f32[4,1,512]{2,1,0:T(1,128)} %bitcast.12, bf16[2048,1536]{1,0:T(8,128)(2,1)} %get-tuple-element.7.gateg_ref, bf16[256,1536]{1,0:T(8,128)(2,1)} %up_ref.1, ...), custom_call_target="tpu_custom_call" | custom-call | flops 11000000512 | bytes 40000000 | tf_op jit(solution)/shard_map/project_and_feed/pallas_call | solution.py:763
  199.9 1.9 slice.14
  201.8 1.3 slice.15
  (9 shorter events, 0.1 us)
Async XLA Ops:
  0.6 1.9 copy-start.11
  1.3 1.5 copy-start.5
  3.5 0.7 copy-start.12
  3.5 0.7 copy-start.10
  3.5 0.7 copy-start.8
  3.5 1.1 copy-start
  3.5 1.3 copy-start.1
  3.6 1.3 copy-start.2
  4.9 49.0 %copy-start.6 = (bf16[512,512]{1,0:T(8,128)(2,1)S(1)}, bf16[512,512]{1,0:T(8,128)(2,1)}, u32[]{:S(2)}) copy-start(bf16[512,512]{1,0:T(8,128)(2,1)} %param.25) | copy-start | bytes 1572868
  4.9 49.0 %copy-start.7 = (bf16[3,512]{1,0:T(4,128)(2,1)S(1)}, bf16[3,512]{1,0:T(4,128)(2,1)}, u32[]{:S(2)}) copy-start(bf16[3,512]{1,0:T(4,128)(2,1)} %param.26) | copy-start | bytes 9220
  4.9 49.9 %copy-start.9 = (bf16[2048]{0:T(1024)(128)(2,1)S(1)}, bf16[2048]{0:T(1024)(128)(2,1)}, u32[]{:S(2)}) copy-start(bf16[2048]{0:T(1024)(128)(2,1)} %param.28) | copy-start | bytes 12292
  51.7 1.4 copy-start.3
  53.0 0.9 copy-start.4
